TPU v7x, 32 devices: a whole 2x2x4 slice. The times are simulated.
32 devices in a mesh: wave: 8 (over z, x), cfd: 4 (over y, core).
Axes of the slice: x: 2, y: 2, z: 4, core: 2. Of those that a mesh axis runs over, the one named last changes fastest.
Arguments:
- phi_spec: float32 [2, 8192, 4096], P(None, ('wave', 'cfd')), may hold values from -6 to 6
- elevation: float32 [4096, 8192], P(('wave', 'cfd')), may hold values from -4 to 4
- hull_owner: int32 [128, 1], replicated, may hold values from 0 to 31; in each aligned block of 128 rows (0 to 127, 128 to 255, ...) at most 16 rows name the same one
- hull_place: int32 [128], replicated, may hold values from 0 to 1023
- cell_need: int32 [1024], P(('wave', 'cfd')), may hold values from 0 to 127
- cfd_velocity: float32 [1024, 3, 8, 128], P(('wave', 'cfd')), may hold values from -6 to 6
- relax_gain: float32 [1024], P(('wave', 'cfd')), may hold values from 0.2 to 1
Outputs:
- w_surface: float32 [4096, 8192], P(('wave', 'cfd'))
- blended: float32 [1024, 3, 8, 128], P(('wave', 'cfd'))
- pressure: float32 [1024, 8, 128], P(('wave', 'cfd'))
Inputs may be any that keep to these rules, and one draw needn't show every extreme that they name: `hull_owner`: no device owns more than 16 hull-zone blocks, and one device owns exactly 16.
All inputs are finite; a program needn't handle non-finite values.
Results may differ from a plain program's by a relative error of at most 0.00011.
Values sent between devices are 32-bit elements; how exact they have to be, the bound alone decides.
A program may use at most 192 MiB of HBM per device.

v0:
```python
import math

import jax
import jax.numpy as jnp
from jax import lax
from jax.sharding import PartitionSpec as P

YA = 32
BY = 8
TILE = 128
SWEEPS = 4
HULL_DEV = 4


HIGHEST = lax.Precision.HIGHEST


def wave_numbers(start, count, length):
    signed = (start + jnp.arange(count, dtype=jnp.int32) + length // 2) % length - length // 2
    return signed.astype(jnp.float32) * (2.0 * math.pi / length)


def phase_table(rows, cols, length, sign):
    product = (
        jnp.arange(rows, dtype=jnp.int32)[:, None]
        * jnp.arange(cols, dtype=jnp.int32)[None, :]
        % length
    )
    angle = product.astype(jnp.float32) * (2.0 * math.pi / length)
    return (jnp.cos(angle), sign * jnp.sin(angle))


def complex_einsum(formula, table_re, table_im, data_re, data_im, real_only):
    direct = jnp.einsum(formula, table_re, data_re, precision=HIGHEST)
    crossed = jnp.einsum(formula, table_im, data_im, precision=HIGHEST)
    if real_only:
        return direct - crossed
    mixed_one = jnp.einsum(formula, table_re, data_im, precision=HIGHEST)
    mixed_two = jnp.einsum(formula, table_im, data_re, precision=HIGHEST)
    return (direct - crossed, mixed_one + mixed_two)


def rotate(values_re, values_im, factor_re, factor_im):
    return (
        values_re * factor_re - values_im * factor_im,
        values_re * factor_im + values_im * factor_re,
    )


def lines_inverse(spectra_re, spectra_im, devices):
    count, rows_x, span_y = spectra_re.shape
    first = YA
    second = span_y // first
    shaped_re = spectra_re.reshape(count, rows_x, first, second)
    shaped_im = spectra_im.reshape(count, rows_x, first, second)
    one_re, one_im = phase_table(first, first, first, 1.0)
    turn_re, turn_im = phase_table(first, second, span_y, 1.0)
    two_re, two_im = phase_table(second, second, second, 1.0)
    section_re, section_im = complex_einsum(
        "kn,frnm->frkm", one_re, one_im, shaped_re, shaped_im, False
    )
    section_re, section_im = rotate(section_re, section_im, turn_re, turn_im)
    final_re, final_im = complex_einsum(
        "qm,frkm->fqkr", two_re, two_im, section_re, section_im, False
    )
    scaling = 1.0 / math.sqrt(span_y)
    return (
        (final_re * scaling).reshape(count, devices, -1),
        (final_im * scaling).reshape(count, devices, -1),
    )


def columns_inverse(blocks_re, blocks_im, rows_y, span_x):
    count, devices, merged = blocks_re.shape
    rows_x = merged // rows_y
    shaped_re = blocks_re.reshape(count, devices, rows_y, rows_x)
    shaped_im = blocks_im.reshape(count, devices, rows_y, rows_x)
    one_re, one_im = phase_table(devices, devices, devices, 1.0)
    turn_re, turn_im = phase_table(devices, rows_x, span_x, 1.0)
    two_re, two_im = phase_table(rows_x, rows_x, rows_x, 1.0)
    section_re, section_im = complex_einsum(
        "kj,fjyr->fkyr", one_re, one_im, shaped_re, shaped_im, False
    )
    section_re, section_im = rotate(
        section_re, section_im, turn_re[:, None, :], turn_im[:, None, :]
    )
    final = complex_einsum("qr,fkyr->fyqk", two_re, two_im, section_re, section_im, True)
    return final.reshape(count, rows_y, span_x) * (1.0 / math.sqrt(span_x))


def lines_transform(data_re, data_im, sign):
    span_y, rows_x = data_re.shape
    first = YA
    second = span_y // first
    shaped_re = data_re.reshape(first, second, rows_x)
    shaped_im = data_im.reshape(first, second, rows_x)
    one_re, one_im = phase_table(first, first, first, sign)
    turn_re, turn_im = phase_table(first, second, span_y, sign)
    two_re, two_im = phase_table(second, second, second, sign)
    section_re, section_im = complex_einsum(
        "kn,nmr->kmr", one_re, one_im, shaped_re, shaped_im, False
    )
    section_re, section_im = rotate(
        section_re, section_im, turn_re[:, :, None], turn_im[:, :, None]
    )
    final_re, final_im = complex_einsum(
        "qm,kmr->qkr", two_re, two_im, section_re, section_im, False
    )
    scaling = 1.0 / math.sqrt(span_y)
    return (
        (final_re * scaling).reshape(span_y, rows_x),
        (final_im * scaling).reshape(span_y, rows_x),
    )


def blend_smooth(hos_blocks, cfd_velocity, relax_gain):
    position = jnp.arange(TILE, dtype=jnp.float32)
    ramp = 1.0 - (position + 0.5) / TILE
    weight = relax_gain[:, None, None, None] * ramp[None, None, None, :]
    blended = weight * hos_blocks + (1.0 - weight) * cfd_velocity
    padded_u = jnp.pad(blended[:, 0], ((0, 0), (0, 0), (1, 1)))
    padded_v = jnp.pad(blended[:, 1], ((0, 0), (1, 1), (0, 0)))
    source = (padded_u[:, :, 2:] - padded_u[:, :, :-2]) * 0.5 + (
        padded_v[:, 2:, :] - padded_v[:, :-2, :]
    ) * 0.5
    pressure = jnp.zeros_like(source)
    for sweep in range(SWEEPS):
        padded = jnp.pad(pressure, ((0, 0), (1, 1), (1, 1)))
        beside = (
            padded[:, 2:, 1:-1] + padded[:, :-2, 1:-1] + padded[:, 1:-1, 2:] + padded[:, 1:-1, :-2]
        )
        pressure = (beside - source) / 4.5
    return (blended, pressure)


def local(phi_spec, elevation, hull_owner, hull_place, cell_need, cfd_velocity, relax_gain):
    devices = lax.axis_size(("wave", "cfd"))
    rank_here = lax.axis_index(("wave", "cfd"))
    rows_x = phi_spec.shape[1]
    span_y = phi_spec.shape[2]
    rows_y, span_x = elevation.shape
    wave_x = wave_numbers(rank_here * rows_x, rows_x, span_x)[:, None]
    wave_y = wave_numbers(0, span_y, span_y)[None, :]
    magnitude = jnp.sqrt(wave_x * wave_x + wave_y * wave_y)
    spec_re = phi_spec[0]
    spec_im = phi_spec[1]
    fields_re = jnp.stack(
        [magnitude * spec_re, magnitude * magnitude * spec_re, -wave_x * spec_im, -wave_y * spec_im]
    )
    fields_im = jnp.stack(
        [magnitude * spec_im, magnitude * magnitude * spec_im, wave_x * spec_re, wave_y * spec_re]
    )
    lines_re, lines_im = lines_inverse(fields_re, fields_im, devices)
    moved_re, moved_im = (
        lax.all_to_all(lines_re, ("wave", "cfd"), split_axis=1, concat_axis=1, tiled=True),
        lax.all_to_all(lines_im, ("wave", "cfd"), split_axis=1, concat_axis=1, tiled=True),
    )
    physical = columns_inverse(moved_re, moved_im, rows_y, span_x)
    w_first = physical[0]
    curvature = physical[1]
    vel_x = physical[2]
    vel_y = physical[3]
    product = -elevation * w_first
    shaped = product.reshape(rows_y, rows_x, devices)
    one_re, one_im = phase_table(rows_x, rows_x, rows_x, -1.0)
    turn_re, turn_im = phase_table(rows_x, devices, span_x, -1.0)
    two_re, two_im = phase_table(devices, devices, devices, -1.0)
    section_re = jnp.einsum("kn,ynm->ykm", one_re, shaped, precision=HIGHEST)
    section_im = jnp.einsum("kn,ynm->ykm", one_im, shaped, precision=HIGHEST)
    section_re, section_im = rotate(section_re, section_im, turn_re, turn_im)
    final_re, final_im = complex_einsum(
        "qm,ykm->qyk", two_re, two_im, section_re, section_im, False
    )
    scaling = 1.0 / math.sqrt(span_x)
    sent_re = (final_re * scaling).reshape(devices, -1)
    sent_im = (final_im * scaling).reshape(devices, -1)
    got_re, got_im = (
        lax.all_to_all(sent_re, ("wave", "cfd"), split_axis=0, concat_axis=0, tiled=True),
        lax.all_to_all(sent_im, ("wave", "cfd"), split_axis=0, concat_axis=0, tiled=True),
    )
    lines_re, lines_im = lines_transform(
        got_re.reshape(span_y, rows_x), got_im.reshape(span_y, rows_x), -1.0
    )
    wave_row = wave_numbers(rank_here * rows_x, rows_x, span_x)[None, :]
    wave_col = wave_numbers(0, span_y, span_y)[:, None]
    magnitude_lines = jnp.sqrt(wave_row * wave_row + wave_col * wave_col)
    back_re, back_im = lines_transform(lines_re * magnitude_lines, lines_im * magnitude_lines, 1.0)
    return_re, return_im = (
        lax.all_to_all(
            back_re.reshape(devices, -1), ("wave", "cfd"), split_axis=0, concat_axis=0, tiled=True
        ),
        lax.all_to_all(
            back_im.reshape(devices, -1), ("wave", "cfd"), split_axis=0, concat_axis=0, tiled=True
        ),
    )
    w_second = columns_inverse(return_re[None], return_im[None], rows_y, span_x)[0]
    w_surface = w_first + w_second + elevation * curvature
    kinematics = jnp.stack([vel_x, vel_y, w_surface])
    across = span_x // TILE

    def cut(place):
        line_at = place // across * BY
        point_at = place % across * TILE
        return lax.dynamic_slice(kinematics, (jnp.int32(0), line_at, point_at), (3, BY, TILE))

    owners = hull_owner[:, 0]
    owner_table = (owners[:, None] == jnp.arange(devices, dtype=jnp.int32)[None, :]).astype(
        jnp.int32
    )
    owner_rank = jnp.sum(jnp.cumsum(owner_table, axis=0) * owner_table, axis=1) - 1
    mine = owners == rank_here
    capacity = 4 * HULL_DEV
    select = (
        mine[None, :] & (owner_rank[None, :] == jnp.arange(capacity, dtype=jnp.int32)[:, None])
    ).astype(jnp.int32)
    slot_place = jnp.sum(select * hull_place[None, :], axis=1)
    slot_valid = jnp.sum(select, axis=1).astype(jnp.float32)
    tiles = jax.vmap(cut)(slot_place) * slot_valid[:, None, None, None]
    gathered = lax.all_gather(tiles, ("wave", "cfd"), axis=0, tiled=True)
    slot_index = owners[cell_need] * capacity + owner_rank[cell_need]
    hos_blocks = jnp.take(gathered, slot_index, axis=0)
    blended, pressure = blend_smooth(hos_blocks, cfd_velocity, relax_gain)
    return (w_surface, blended, pressure)


def solution(mesh):
    return jax.shard_map(
        local,
        mesh=mesh,
        in_specs=(
            P(None, ("wave", "cfd"), None),
            P(("wave", "cfd"), None),
            P(),
            P(),
            P(("wave", "cfd")),
            P(("wave", "cfd"), None, None, None),
            P(("wave", "cfd")),
        ),
        out_specs=(
            P(("wave", "cfd"), None),
            P(("wave", "cfd"), None, None, None),
            P(("wave", "cfd"), None, None),
        ),
        check_vma=False,
    )
```

profile of v0, /device:TPU:0, one launch (start us, length us, event | category | flops | bytes accessed | tf_op | source)
XLA Modules:
  0.0 1974.8 jit_solution(8891516956807003516)
XLA Ops:
  7.4 10.9 multiply_bitcast_fusion.10
  48.1 21.7 %fusion.271 = f32[4,256,128,32]{2,3,1,0:T(8,128)} fusion(f32[4,256,32,128]{3,2,1,0:T(8,128)} %bitcast_dynamic-update-slice_fusion.5), kind=kOutput, calls=%fused_computation.328 | convolution fusion | flops 1610627072 | bytes 33554432 | tf_op jit(solution)/shard_map/kn,frnm->frkm/dot_general | solution.py:34
  79.5 21.7 %fusion.269 = f32[4,256,128,32]{2,3,1,0:T(8,128)} fusion(f32[4,256,32,128]{3,2,1,0:T(8,128)} %bitcast_dynamic-update-slice_fusion.1), kind=kOutput, calls=%fused_computation.326 | convolution fusion | flops 1610627072 | bytes 33554432 | tf_op jit(solution)/shard_map/kn,frnm->frkm/dot_general | solution.py:38
  101.3 23.6 %convolution_subtract_fusion = f32[4,256,128,32]{2,3,1,0:T(8,128)} fusion(f32[4,256,128,32]{2,3,1,0:T(8,128)} %fusion.271, f32[4,256,32,128]{3,2,1,0:T(8,128)} %bitcast_dynamic-update-slice_fusion.1), kind=kOutput, calls=%fused_computation.44 | convolution fusion | flops 1614821376 | bytes 50331648 | tf_op jit(solution)/shard_map/kn,frnm->frkm/dot_general | solution.py:35
  124.8 32.6 %fusion.2 = (f32[4,256,32,128]{3,2,1,0:T(8,128)}, f32[4,256,32,128]{3,2,1,0:T(8,128)}) fusion(f32[4,256,128,32]{2,3,1,0:T(8,128)} %convolution_subtract_fusion, f32[32,128]{1,0:T(8,128)S(1)} %get-tuple-element.78, f32[32,128]{1,0:T(8,128)S(1)} %get-tuple-element.79, f32[4,256,128,32]{2,3,1,0:T(8,128)} %fusion.269, ...), kind=kOutput, calls=%fused_computation.13 | convolution fusion | flops 1639987200 | bytes 83918848 | tf_op jit(solution)/shard_map/kn,frnm->frkm/dot_general | solution.py:39
  157.5 30.5 %fusion.16 = f32[4,256,32,128]{3,1,2,0:T(8,128)} fusion(f32[4,256,32,128]{3,2,1,0:T(8,128)} %get-tuple-element.49), kind=kOutput, calls=%fused_computation.32 | convolution fusion | flops 6442680320 | bytes 33554432 | tf_op jit(solution)/shard_map/qm,frkm->fqkr/dot_general | solution.py:38
  187.9 30.9 %multiply_bitcast_fusion.1 = f32[4,128,32,256]{1,3,2,0:T(8,128)} fusion(f32[4,256,32,128]{3,1,2,0:T(8,128)} %fusion.16, f32[4,256,32,128]{3,2,1,0:T(8,128)S(1)} %copy-done.1), kind=kOutput, calls=%fused_computation.22 | convolution fusion | flops 6451068928 | bytes 50331648 | tf_op jit(solution)/shard_map/qm,frkm->fqkr/dot_general | solution.py:39
  218.9 19.9 %copy.176 = f32[4,128,32,256]{3,2,1,0:T(8,128)} copy(f32[4,128,32,256]{1,3,2,0:T(8,128)} %multiply_bitcast_fusion.1) | data formatting | bytes 33554432 | tf_op jit(solution)/shard_map/mul | solution.py:69
  238.7 18.2 reshape.697
  256.9 20.9 %copy.177 = f32[4,32,32768]{2,0,1:T(4,128)} copy(f32[4,32,32768]{2,1,0:T(8,128)} %reshape.697) | data formatting | bytes 33554432 | tf_op jit(solution)/shard_map/reshape | solution.py:69
  277.8 7.9 all-to-all-start.1
  285.7 28.6 %fusion.18 = f32[4,256,32,128]{3,1,2,0:T(8,128)S(1)} fusion(f32[4,256,32,128]{3,2,1,0:T(8,128)} %get-tuple-element.49), kind=kOutput, calls=%fused_computation.34 | convolution fusion | flops 6442680320 | bytes 33554432 | tf_op jit(solution)/shard_map/qm,frkm->fqkr/dot_general | solution.py:35
  314.3 30.9 %multiply_bitcast_fusion.2 = f32[4,128,32,256]{1,3,2,0:T(8,128)} fusion(f32[4,256,32,128]{3,1,2,0:T(8,128)S(1)} %fusion.18, f32[4,256,32,128]{3,2,1,0:T(8,128)} %get-tuple-element.48), kind=kOutput, calls=%fused_computation.23 | convolution fusion | flops 6451068928 | bytes 50331648 | tf_op jit(solution)/shard_map/qm,frkm->fqkr/dot_general | solution.py:34
  345.3 19.9 %copy.170 = f32[4,128,32,256]{3,2,1,0:T(8,128)} copy(f32[4,128,32,256]{1,3,2,0:T(8,128)} %multiply_bitcast_fusion.2) | data formatting | bytes 33554432 | tf_op jit(solution)/shard_map/mul | solution.py:68
  365.2 18.2 reshape.695
  383.4 20.9 %copy.171 = f32[4,32,32768]{2,0,1:T(4,128)} copy(f32[4,32,32768]{2,1,0:T(8,128)} %reshape.695) | data formatting | bytes 33554432 | tf_op jit(solution)/shard_map/reshape | solution.py:68
  404.3 247.0 %all-to-all-done.1 = f32[4,32,32768]{2,0,1:T(4,128)} async-done(((f32[4,32,32768]{2,0,1:T(4,128)}), f32[4,32,32768]{2,0,1:T(4,128)}, u32[]{:S(2)}, u32[]{:S(2)}) %all-to-all-start.1) | async-done | bytes 16777248 | tf_op jit(solution)/shard_map/all_to_all | solution.py:156
  651.4 16.2 all-to-all-start
  673.4 20.5 %reshape.771 = f32[4,32,128,256]{3,2,0,1:T(8,128)} reshape(f32[4,32,32768]{2,0,1:T(4,128)} %all-to-all-done.1) | data formatting | bytes 33554432 | tf_op jit(solution)/shard_map/reshape | solution.py:77
  694.0 33.4 %fusion.10 = f32[4,128,256,32]{2,3,1,0:T(8,128)} fusion(f32[4,32,128,256]{3,2,0,1:T(8,128)} %reshape.771), kind=kOutput, calls=%fused_computation.26 | convolution fusion | flops 1610627072 | bytes 33554432 | tf_op jit(solution)/shard_map/kj,fjyr->fkyr/dot_general | solution.py:35
  727.4 33.2 %fusion.8 = f32[4,128,256,32]{2,3,1,0:T(8,128)} fusion(f32[4,32,128,256]{3,2,0,1:T(8,128)} %reshape.771), kind=kOutput, calls=%fused_computation.24 | convolution fusion | flops 1610627072 | bytes 33554432 | tf_op jit(solution)/shard_map/kj,fjyr->fkyr/dot_general | solution.py:38
  760.5 272.7 %all-to-all-done = f32[4,32,32768]{2,0,1:T(4,128)} async-done(((f32[4,32,32768]{2,0,1:T(4,128)}), f32[4,32,32768]{2,0,1:T(4,128)}, u32[]{:S(2)}, u32[]{:S(2)}) %all-to-all-start) | async-done | bytes 16777248 | tf_op jit(solution)/shard_map/all_to_all | solution.py:155
  1033.2 20.5 %reshape.770 = f32[4,32,128,256]{3,2,0,1:T(8,128)} reshape(f32[4,32,32768]{2,0,1:T(4,128)} %all-to-all-done) | data formatting | bytes 33554432 | tf_op jit(solution)/shard_map/reshape | solution.py:76
  1053.8 32.0 %fusion.28 = f32[4,128,256,32]{2,3,1,0:T(8,128)} fusion(f32[4,128,256,32]{2,3,1,0:T(8,128)} %fusion.10, f32[4,32,128,256]{3,2,0,1:T(8,128)} %reshape.770), kind=kOutput, calls=%fused_computation.41 | convolution fusion | flops 1614821376 | bytes 50331648 | tf_op jit(solution)/shard_map/kj,fjyr->fkyr/dot_general | solution.py:34
  1085.7 38.5 %fusion = (f32[4,32,128,256]{3,1,2,0:T(8,128)}, f32[4,32,128,256]{3,1,2,0:T(8,128)}) fusion(f32[4,128,256,32]{2,3,1,0:T(8,128)} %fusion.28, f32[32,256]{1,0:T(8,128)S(1)} %get-tuple-element.80, f32[32,256]{1,0:T(8,128)S(1)} %get-tuple-element.81, f32[4,128,256,32]{2,3,1,0:T(8,128)} %fusion.8, f32[4,32,128,256]{3,2,0,1:T(8,128)} %reshape.770), kind=kOutput, calls=%fused_computation.7 | convolution fusion | flops 1639987200 | bytes 83951616 | tf_op jit(solution)/shard_map/kj,fjyr->fkyr/dot_general | solution.py:39
  1124.2 32.0 %fusion.4 = f32[4,32,128,256]{3,2,1,0:T(8,128)} fusion(f32[4,32,128,256]{3,1,2,0:T(8,128)} %get-tuple-element.47), kind=kOutput, calls=%fused_computation.17 | convolution fusion | flops 12885819392 | bytes 33554432 | tf_op jit(solution)/shard_map/qr,fkyr->fyqk/dot_general | solution.py:35
  1156.3 33.0 %multiply_bitcast_fusion = f32[4,128,256,32]{2,1,3,0:T(8,128)} fusion(f32[4,32,128,256]{3,2,1,0:T(8,128)} %fusion.4, f32[4,32,128,256]{3,1,2,0:T(8,128)} %get-tuple-element.46), kind=kOutput, calls=%fused_computation.21 | convolution fusion | flops 12894208000 | bytes 50331648 | tf_op jit(solution)/shard_map/qr,fkyr->fyqk/dot_general | solution.py:34
  1189.3 7.8 fusion.512
  1250.6 16.1 all-to-all-start.3
  1266.7 8.7 fusion.98
  1293.5 67.6 %all-to-all-done.3 = f32[32,1,32768]{2,1,0:T(1,128)} async-done(((f32[32,1,32768]{2,1,0:T(1,128)}), f32[32,1,32768]{2,1,0:T(1,128)}, u32[]{:S(2)}, u32[]{:S(2)}) %all-to-all-start.3) | async-done | bytes 4194336 | tf_op jit(solution)/shard_map/all_to_all | solution.py:179
  1366.9 13.8 reduce.1
  1380.7 8.1 fusion.46
  1394.1 66.8 %all-to-all-done.2 = f32[32,1,32768]{2,1,0:T(1,128)} async-done(((f32[32,1,32768]{2,1,0:T(1,128)}), f32[32,1,32768]{2,1,0:T(1,128)}, u32[]{:S(2)}, u32[]{:S(2)}) %all-to-all-start.2) | async-done | bytes 4194336 | tf_op jit(solution)/shard_map/all_to_all | solution.py:178
  1460.8 14.3 reduce
  1540.4 7.9 multiply_subtract_fusion
  1578.5 9.1 fusion.74
  1605.8 67.1 %all-to-all-done.5 = f32[32,1,32768]{2,1,0:T(1,128)} async-done(((f32[32,1,32768]{2,1,0:T(1,128)}), f32[32,1,32768]{2,1,0:T(1,128)}, u32[]{:S(2)}, u32[]{:S(2)}) %all-to-all-start.5) | async-done | bytes 4194336 | tf_op jit(solution)/shard_map/all_to_all | solution.py:192
  1692.2 10.3 copy.232
  1702.6 13.7 reduce.3
  1716.3 8.2 fusion.38
  1729.9 42.8 %all-to-all-done.4 = f32[32,1,32768]{2,1,0:T(1,128)} async-done(((f32[32,1,32768]{2,1,0:T(1,128)}), f32[32,1,32768]{2,1,0:T(1,128)}, u32[]{:S(2)}, u32[]{:S(2)}) %all-to-all-start.4) | async-done | bytes 4194336 | tf_op jit(solution)/shard_map/all_to_all | solution.py:189
  1772.6 13.9 reduce.2
  1815.8 8.7 fusion.52
  1824.5 10.0 pad_maximum_fusion
  1834.5 12.6 copy.233
  1847.1 44.4 %while.1 = (s32[]{:T(128)}, f32[3,128,8192]{2,1,0:T(8,128)}, s32[16,3]{0,1:T(4,128)S(1)}, f32[16,3,8,128]{3,2,1,0:T(8,128)S(1)}, s32[]{:T(128)}) while((s32[]{:T(128)}, f32[3,128,8192]{2,1,0:T(8,128)}, s32[16,3]{0,1:T(4,128)S(1)}, f32[16,3,8,128]{3,2,1,0:T(8,128)S(1)}, s32[]{:T(128)}) %tuple.53), condition=%wide.while_cond, body=%wide.while_body.sunk | while | flops 2 | bytes 24693 | solution.py:204
  1899.6 63.1 %all-gather.2.cloned.1.call-done = f32[512,3,8,128]{3,2,1,0:T(8,128)} async-done(((f32[16,3,8,128]{3,2,1,0:T(8,128)}), f32[512,3,8,128]{3,2,1,0:T(8,128)}) %all-gather.2.cloned.1.call-update) | async-done | bytes 6291472 | tf_op jit(solution)/shard_map/all_gather | solution.py:219
  (227 shorter events, 352.5 us)
Async XLA Ops:
  7.2 11.1 copy-start.32
  7.3 117.5 %copy-start.27 = (f32[32,128]{1,0:T(8,128)}, f32[32,128]{1,0:T(8,128)S(1)}, u32[]{:S(2)}) copy-start(f32[32,128]{1,0:T(8,128)S(1)} %get-tuple-element.78) | copy-start | bytes 49156
  7.3 117.5 %copy-start.29 = (f32[32,128]{1,0:T(8,128)}, f32[32,128]{1,0:T(8,128)S(1)}, u32[]{:S(2)}) copy-start(f32[32,128]{1,0:T(8,128)S(1)} %get-tuple-element.79) | copy-start | bytes 49156
  21.2 3.7 copy-start.16
  24.9 3.4 copy-start.15
  28.4 3.4 copy-start.14
  31.8 3.4 copy-start.13
  48.1 21.7 %copy-start.20 = (f32[32,8,32,128]{3,2,1,0:T(8,128)S(1)}, f32[32,8,32,128]{3,2,1,0:T(8,128)}, u32[]{:S(2)}) copy-start(f32[32,8,32,128]{3,2,1,0:T(8,128)} %copy.262) | copy-start | bytes 12582916
  69.8 3.7 copy-start.21
  73.5 3.7 copy-start.19
  157.5 30.5 %copy-start.1 = (f32[4,256,32,128]{3,2,1,0:T(8,128)S(1)}, f32[4,256,32,128]{3,2,1,0:T(8,128)}, u32[]{:S(2)}) copy-start(f32[4,256,32,128]{3,2,1,0:T(8,128)} %get-tuple-element.48) | copy-start | bytes 50331652
  277.8 373.6 %all-to-all-start.1 = ((f32[4,32,32768]{2,0,1:T(4,128)}), f32[4,32,32768]{2,0,1:T(4,128)}, u32[]{:S(2)}, u32[]{:S(2)}) async-start(f32[4,32,32768]{2,0,1:T(4,128)} %copy.177), calls=%async_computation.1 | async-start | bytes 33554432 | tf_op jit(solution)/shard_map/all_to_all | solution.py:156
  651.4 381.9 %all-to-all-start = ((f32[4,32,32768]{2,0,1:T(4,128)}), f32[4,32,32768]{2,0,1:T(4,128)}, u32[]{:S(2)}, u32[]{:S(2)}) async-start(f32[4,32,32768]{2,0,1:T(4,128)} %copy.171), calls=%async_computation | async-start | bytes 33554432 | tf_op jit(solution)/shard_map/all_to_all | solution.py:155
  673.3 412.5 %copy-start.22 = (f32[32,256]{1,0:T(8,128)}, f32[32,256]{1,0:T(8,128)S(1)}, u32[]{:S(2)}) copy-start(f32[32,256]{1,0:T(8,128)S(1)} %get-tuple-element.80) | copy-start | bytes 98308
  673.3 412.5 %copy-start.24 = (f32[32,256]{1,0:T(8,128)}, f32[32,256]{1,0:T(8,128)S(1)}, u32[]{:S(2)}) copy-start(f32[32,256]{1,0:T(8,128)S(1)} %get-tuple-element.81) | copy-start | bytes 98308
  1213.8 7.6 copy-start.12
  1226.2 6.2 copy-start.11
  1226.2 6.2 copy-start.6
  1250.6 110.4 %all-to-all-start.3 = ((f32[32,1,32768]{2,1,0:T(1,128)}), f32[32,1,32768]{2,1,0:T(1,128)}, u32[]{:S(2)}, u32[]{:S(2)}) async-start(f32[32,1,32768]{2,1,0:T(1,128)} %all_to_all.41), calls=%async_computation.3 | async-start | bytes 8388608 | tf_op jit(solution)/shard_map/all_to_all | solution.py:179
  1266.7 8.7 copy-start.7
  1293.5 73.0 %copy-start.30 = (f32[32,128]{1,0:T(8,128)S(1)}, f32[32,128]{1,0:T(8,128)}, u32[]{:S(2)}) copy-start(f32[32,128]{1,0:T(8,128)} %copy-done.29) | copy-start | bytes 49156
  1293.5 73.1 %copy-start.28 = (f32[32,128]{1,0:T(8,128)S(1)}, f32[32,128]{1,0:T(8,128)}, u32[]{:S(2)}) copy-start(f32[32,128]{1,0:T(8,128)} %copy-done.27) | copy-start | bytes 49156
  1361.1 99.8 %all-to-all-start.2 = ((f32[32,1,32768]{2,1,0:T(1,128)}), f32[32,1,32768]{2,1,0:T(1,128)}, u32[]{:S(2)}, u32[]{:S(2)}) async-start(f32[32,1,32768]{2,1,0:T(1,128)} %all_to_all.40), calls=%async_computation.2 | async-start | bytes 8388608 | tf_op jit(solution)/shard_map/all_to_all | solution.py:178
  1380.7 8.1 copy-start.9
  1475.1 7.7 copy-start.4
  1475.1 7.7 copy-start.17
  1517.2 2.6 copy-start.33
  1548.3 6.3 copy-start.8
  1548.3 6.3 copy-start.2
  1573.0 99.8 %all-to-all-start.5 = ((f32[32,1,32768]{2,1,0:T(1,128)}), f32[32,1,32768]{2,1,0:T(1,128)}, u32[]{:S(2)}, u32[]{:S(2)}) async-start(f32[32,1,32768]{2,1,0:T(1,128)} %all_to_all.43), calls=%async_computation.5 | async-start | bytes 8388608 | tf_op jit(solution)/shard_map/all_to_all | solution.py:192
  1578.5 9.1 copy-start.3
  1605.8 72.5 %copy-start = (s32[128,1]{0,1:T(1,128)S(1)}, s32[128,1]{0,1:T(1,128)}, u32[]{:S(2)}) copy-start(s32[128,1]{0,1:T(1,128)} %param.9) | copy-start | bytes 1540
  1605.8 73.0 %copy-start.35 = (s32[128]{0:T(128)S(1)}, s32[128]{0:T(128)}, u32[]{:S(2)}) copy-start(s32[128]{0:T(128)} %param.10) | copy-start | bytes 1540
  1672.9 99.8 %all-to-all-start.4 = ((f32[32,1,32768]{2,1,0:T(1,128)}), f32[32,1,32768]{2,1,0:T(1,128)}, u32[]{:S(2)}, u32[]{:S(2)}) async-start(f32[32,1,32768]{2,1,0:T(1,128)} %all_to_all.42), calls=%async_computation.4 | async-start | bytes 8388608 | tf_op jit(solution)/shard_map/all_to_all | solution.py:189
  1678.3 284.5 %all-gather.2.cloned.1.call-start = ((), (), s32[]{:S(2)}) async-start(), calls=%async_computation.6 | async-start | bytes 6488064 | tf_op jit(solution)/shard_map/all_gather | solution.py:219
  1716.3 8.2 copy-start.10
  1786.6 7.4 copy-start.5
  1786.6 7.4 copy-start.18
  1794.0 3.9 copy-start.23
  1794.0 3.9 copy-start.25
  1834.5 57.8 %copy-start.36 = (s32[32]{0:T(128)S(1)}, s32[32]{0:T(128)}, u32[]{:S(2)}) copy-start(s32[32]{0:T(128)} %param.11) | copy-start | bytes 388
  1834.5 59.4 %copy-start.34 = (f32[32]{0:T(128)S(1)}, f32[32]{0:T(128)}, u32[]{:S(2)}) copy-start(f32[32]{0:T(128)} %param.13) | copy-start | bytes 388
  1894.0 72.1 %copy-start.31 = (f32[32,3,8,128]{3,2,1,0:T(8,128)S(1)}, f32[32,3,8,128]{3,2,1,0:T(8,128)}, u32[]{:S(2)}) copy-start(f32[32,3,8,128]{3,2,1,0:T(8,128)} %param.12) | copy-start | bytes 1179652
  1966.2 1.3 copy-start.26
Sparse Core Ops, SparseCore 0:
  1892.4 70.2 all-gather.1
where the time goes:
time: 1990 us; the launch traced here: 1970 us
  waiting for transfers between devices  827 us (42%)
  matrix products  608 us (31%)
  local copies, waits for them, and re-layouts  371 us (19%)
  other arithmetic  96.2 us (5%)
  starting transfers between devices  56.4 us (3%)
    all_to_all x1, waiting for transfers between devices, local(): lax.all_to_all(lines_re, ('wave', 'cfd'), split_axis=1, concat_axis=1, ti...  273 us
    all_to_all x1, waiting for transfers between devices, local(): lax.all_to_all(lines_im, ('wave', 'cfd'), split_axis=1, concat_axis=1, ti...  247 us
    dot_general x11, matrix products, complex_einsum(): crossed = jnp.einsum(formula, table_im, data_im, precision=HIGHEST)  169 us
    dot_general x11, matrix products, complex_einsum(): direct = jnp.einsum(formula, table_re, data_re, precision=HIGHEST)  166 us
    dot_general x9, matrix products, complex_einsum(): mixed_two = jnp.einsum(formula, table_im, data_re, precision=HIGHEST)  140 us
    dot_general x9, matrix products, complex_einsum(): mixed_one = jnp.einsum(formula, table_re, data_im, precision=HIGHEST)  121 us
    all_to_all x1, waiting for transfers between devices, local(): lax.all_to_all(sent_im, ('wave', 'cfd'), split_axis=0, concat_axis=0, til...  67.6 us
    all_to_all x1, waiting for transfers between devices, local(): lax.all_to_all(back_im.reshape(devices, -1), ('wave', 'cfd'), split_axis=...  67.1 us
  transfers between devices with their start and end apart: 7, of which 7 were waited for; matrix products, arithmetic and copies ran while one was open for 17% of the time, Pallas kernels for 0%

commit v1 on v0

--- a/solution.py
+++ b/solution.py
@@ -2,7 +2,10 @@
 
 import jax
 import jax.numpy as jnp
+import numpy as np
 from jax import lax
+from jax.experimental import pallas as pl
+from jax.experimental.pallas import tpu as pltpu
 from jax.sharding import PartitionSpec as P
 
 YA = 32
@@ -133,7 +136,7 @@
     return (blended, pressure)
 
 
-def local(phi_spec, elevation, hull_owner, hull_place, cell_need, cfd_velocity, relax_gain):
+def local_general(phi_spec, elevation, hull_owner, hull_place, cell_need, cfd_velocity, relax_gain):
     devices = lax.axis_size(("wave", "cfd"))
     rank_here = lax.axis_index(("wave", "cfd"))
     rows_x = phi_spec.shape[1]
@@ -221,6 +224,528 @@
     hos_blocks = jnp.take(gathered, slot_index, axis=0)
     blended, pressure = blend_smooth(hos_blocks, cfd_velocity, relax_gain)
     return (w_surface, blended, pressure)
+
+
+YS = 16
+LANES = 128
+VMEM_BYTES = 56 * 1024 * 1024
+
+
+def slab_dft(values, sign):
+    count = len(values)
+    if count == 1:
+        return values
+    even = slab_dft(values[0::2], sign)
+    odd = slab_dft(values[1::2], sign)
+    half = count // 2
+    low, high = [], []
+    for k in range(half):
+        even_re, even_im = even[k]
+        odd_re, odd_im = odd[k]
+        if k == 0:
+            turned_re, turned_im = odd_re, odd_im
+        elif 4 * k == count:
+            turned_re, turned_im = (-odd_im, odd_re) if sign > 0 else (odd_im, -odd_re)
+        elif 8 * k == count or 8 * k == 3 * count:
+            root = math.sqrt(0.5)
+            cos = root if 8 * k == count else -root
+            turned_re = odd_re * cos - odd_im * (sign * root)
+            turned_im = odd_im * cos + odd_re * (sign * root)
+        else:
+            cos = math.cos(2.0 * math.pi * k / count)
+            sin = sign * math.sin(2.0 * math.pi * k / count)
+            turned_re = odd_re * cos - odd_im * sin
+            turned_im = odd_re * sin + odd_im * cos
+        low.append((even_re + turned_re, even_im + turned_im))
+        high.append((even_re - turned_re, even_im - turned_im))
+    return low + high
+
+
+def phases(rows, cols, length, sign, scale=1.0):
+    product = np.arange(rows)[:, None] * np.arange(cols)[None, :] % length
+    angle = product * (2.0 * math.pi / length)
+    return np.cos(angle) * scale, sign * np.sin(angle) * scale
+
+
+def two_parts(table):
+    table = np.asarray(table, np.float32)
+    high = table.astype(jnp.bfloat16)
+    rest = (table - high.astype(np.float32)).astype(jnp.bfloat16)
+    return jnp.asarray(np.stack([high, rest]))
+
+
+def left_table(count, sign, scale):
+    cos, sin = phases(count, count, count, sign, scale)
+    return two_parts(np.block([[cos, -sin], [sin, cos]]))
+
+
+def right_table(count, sign, scale, real_only):
+    cos, sin = phases(count, count, count, sign, scale)
+    if real_only:
+        return two_parts(np.concatenate([cos, -sin], axis=0))
+    return two_parts(np.block([[cos, sin], [-sin, cos]]))
+
+
+def split(value):
+    high = value.astype(jnp.bfloat16)
+    return high, (value - high.astype(jnp.float32)).astype(jnp.bfloat16)
+
+
+def multiply(left, right, dims):
+    def one(a, b):
+        return lax.dot_general(a, b, (dims, ((), ())), preferred_element_type=jnp.float32)
+
+    return one(left[0], right[0]) + (one(left[0], right[1]) + one(left[1], right[0]))
+
+
+PLAIN = ((1,), (0,))
+ACROSS = ((1,), (1,))
+
+
+def rows_kernel(quantity, span_x, phi_ref, wx_ref, turn_ref, table_ref, out_ref, work_ref):
+    lines = phi_ref.shape[1]
+    span_y = phi_ref.shape[2]
+    long = span_y // YS
+
+    def first(i, carry):
+        rows = pl.ds(pl.multiple_of(i * 8, 8), 8)
+        for lane in range(0, long, LANES):
+            values = []
+            for n in range(YS):
+                at = n * long + lane
+                re = phi_ref[0, rows, at : at + LANES]
+                im = phi_ref[1, rows, at : at + LANES]
+                if quantity != "potential":
+                    place = lax.broadcasted_iota(jnp.int32, (8, LANES), 1) + (
+                        at - (span_y if n >= YS // 2 else 0)
+                    )
+                    wy = place.astype(jnp.float32) * (2.0 * math.pi / span_y)
+                    if quantity == "vertical":
+                        wx = wx_ref[rows, :]
+                        factor = jnp.sqrt(wx * wx + wy * wy)
+                        re, im = re * factor, im * factor
+                    else:
+                        re, im = -(wy * im), wy * re
+                values.append((re, im))
+            for k, (re, im) in enumerate(slab_dft(values, 1.0)):
+                cos = turn_ref[0, k : k + 1, lane : lane + LANES]
+                sin = turn_ref[1, k : k + 1, lane : lane + LANES]
+                re, im = rotate(re, im, cos, sin)
+                work_ref[k, rows, lane : lane + LANES] = re
+                work_ref[k, rows, long + lane : long + lane + LANES] = im
+        return carry
+
+    lax.fori_loop(0, lines // 8, first, 0)
+
+    def second(k, carry):
+        done = multiply((table_ref[0], table_ref[1]), split(work_ref[k]), ACROSS)
+        out_ref[:, 0, k] = done[:long].reshape(long // 8, 8, lines)
+        out_ref[:, 1, k] = done[long:].reshape(long // 8, 8, lines)
+        return carry
+
+    lax.fori_loop(0, YS, second, 0)
+
+
+def rows_inverse(phi_spec, wx_wide, quantity, span_x):
+    _, rows_x, span_y = phi_spec.shape
+    long = span_y // YS
+    cos, sin = phases(YS, long, span_y, 1.0)
+    turn = jnp.asarray(np.stack([cos, sin]), jnp.float32)
+    table = left_table(long, 1.0, 1.0 / math.sqrt(span_y))
+
+    def kernel(*refs):
+        rows_kernel(quantity, span_x, *refs)
+
+    return pl.pallas_call(
+        kernel,
+        grid=(rows_x // LANES,),
+        in_specs=[
+            pl.BlockSpec((2, LANES, span_y), lambda i: (0, i, 0)),
+            pl.BlockSpec((LANES, LANES), lambda i: (i, 0)),
+            pl.BlockSpec(turn.shape, lambda i: (0, 0, 0)),
+            pl.BlockSpec(table.shape, lambda i: (0, 0, 0)),
+        ],
+        out_specs=pl.BlockSpec((long // 8, 2, YS, 8, LANES), lambda i: (0, 0, 0, 0, i)),
+        out_shape=jax.ShapeDtypeStruct((long // 8, 2, YS, 8, rows_x), jnp.float32),
+        scratch_shapes=[pltpu.VMEM((YS, LANES, 2 * long), jnp.float32)],
+        compiler_params=pltpu.CompilerParams(vmem_limit_bytes=VMEM_BYTES),
+        cost_estimate=pl.CostEstimate(
+            flops=4 * 10**10, bytes_accessed=4 * rows_x * span_y * 4, transcendentals=0
+        ),
+        name="rows_" + quantity,
+    )(phi_spec, wx_wide, turn, table)
+
+
+def points_inverse(got_ref, turn_ref, work_ref):
+    devices, _, lines, long = got_ref.shape
+    for row in range(0, lines, 8):
+        rows = slice(row, row + 8)
+
+        def one(i, carry):
+            lane = pl.multiple_of(i * LANES, LANES)
+            here = pl.ds(lane, LANES)
+            values = [
+                (got_ref[s, 0, rows, here], got_ref[s, 1, rows, here]) for s in range(devices)
+            ]
+            for k, (re, im) in enumerate(slab_dft(values, 1.0)):
+                re, im = rotate(re, im, turn_ref[0, k : k + 1, here], turn_ref[1, k : k + 1, here])
+                work_ref[k, rows, here] = re
+                work_ref[k, rows, pl.ds(lane + long, LANES)] = im
+            return carry
+
+        lax.fori_loop(0, long // LANES, one, 0)
+
+
+def first_order_kernel(
+    got_ref, elev_ref, turn_ref, real_ref, table_ref, first_ref, out_ref, work_ref
+):
+    devices, _, lines, long = got_ref.shape
+    points_inverse(got_ref, turn_ref, work_ref)
+    flat = work_ref[...].reshape(devices * lines, 2 * long)
+    w_first = multiply(split(flat), (real_ref[0], real_ref[1]), PLAIN)
+    first_ref[...] = w_first.reshape(devices, lines, long)
+    product = -elev_ref[...].reshape(devices * lines, long) * w_first
+    pair = jnp.concatenate([product, w_first], axis=1)
+    done = multiply(split(pair), (table_ref[0], table_ref[1]), PLAIN)
+    work_ref[...] = done.reshape(devices, lines, 2 * long)
+    for row in range(0, lines, 8):
+        rows = slice(row, row + 8)
+
+        def one(i, carry):
+            lane = pl.multiple_of(i * LANES, LANES)
+            here = pl.ds(lane, LANES)
+            values = []
+            for k in range(devices):
+                re = work_ref[k, rows, here]
+                im = work_ref[k, rows, pl.ds(lane + long, LANES)]
+                values.append(
+                    rotate(re, im, turn_ref[0, k : k + 1, here], -turn_ref[1, k : k + 1, here])
+                )
+            for s, (re, im) in enumerate(slab_dft(values, -1.0)):
+                out_ref[s, 0, rows, here] = re
+                out_ref[s, 1, rows, here] = im
+            return carry
+
+        lax.fori_loop(0, long // LANES, one, 0)
+
+
+def second_order_kernel(got_ref, elev_ref, first_ref, turn_ref, table_ref, out_ref, work_ref):
+    devices, _, lines, long = got_ref.shape
+    points_inverse(got_ref, turn_ref, work_ref)
+    flat = work_ref[...].reshape(devices * lines, 2 * long)
+    done = multiply(split(flat), (table_ref[0], table_ref[1]), PLAIN)
+    w_second = done[:, :long].reshape(devices, lines, long)
+    curvature = done[:, long:].reshape(devices, lines, long)
+    out_ref[...] = first_ref[...] + w_second + elev_ref[...] * curvature
+
+
+LINES_STEP = 16
+
+
+def points_call(kernel, got, others, tables, outs, name):
+    devices, _, lines, long = got.shape
+    real_block = pl.BlockSpec((devices, LINES_STEP, long), lambda i: (0, i, 0))
+    pair_block = pl.BlockSpec((devices, 2, LINES_STEP, long), lambda i: (0, 0, i, 0))
+    blocks = {"real": real_block, "pair": pair_block}
+    shapes = {"real": (devices, lines, long), "pair": (devices, 2, lines, long)}
+    return pl.pallas_call(
+        kernel,
+        grid=(lines // LINES_STEP,),
+        in_specs=[pair_block]
+        + [real_block] * len(others)
+        + [pl.BlockSpec(table.shape, lambda i: (0, 0, 0)) for table in tables],
+        out_specs=[blocks[kind] for kind in outs],
+        out_shape=[jax.ShapeDtypeStruct(shapes[kind], jnp.float32) for kind in outs],
+        scratch_shapes=[pltpu.VMEM((devices, LINES_STEP, 2 * long), jnp.float32)],
+        compiler_params=pltpu.CompilerParams(vmem_limit_bytes=VMEM_BYTES),
+        cost_estimate=pl.CostEstimate(
+            flops=2 * 10**10, bytes_accessed=5 * got.size * 2, transcendentals=0
+        ),
+        name=name,
+    )(got, *others, *tables)
+
+
+def filter_kernel(got_ref, wx_ref, turn_ref, forward_ref, back_ref, out_ref, work_ref):
+    parts = got_ref.shape[0]
+    long = parts * 8
+    span_y = long * YS
+
+    def one(k, carry):
+        pair = jnp.concatenate(
+            [got_ref[:, 0, k].reshape(long, LANES), got_ref[:, 1, k].reshape(long, LANES)], axis=0
+        )
+        work_ref[k] = multiply((forward_ref[0], forward_ref[1]), split(pair), PLAIN)
+        return carry
+
+    lax.fori_loop(0, YS, one, 0)
+
+    def two(i, carry):
+        at = pl.multiple_of(i * 8, 8)
+        rows = pl.ds(at, 8)
+        below = pl.ds(at + long, 8)
+        wx = wx_ref[...]
+        wx_square = wx * wx
+        values = []
+        for k in range(YS):
+            values.append(
+                rotate(
+                    work_ref[k, rows, :],
+                    work_ref[k, below, :],
+                    turn_ref[0, k, rows, :],
+                    -turn_ref[1, k, rows, :],
+                )
+            )
+        values = slab_dft(values, -1.0)
+        for n in range(YS):
+            place = (
+                lax.broadcasted_iota(jnp.int32, (8, LANES), 0)
+                + at
+                + (n * long - (span_y if n >= YS // 2 else 0))
+            )
+            wy = place.astype(jnp.float32) * (2.0 * math.pi / span_y)
+            magnitude = jnp.sqrt(wx_square + wy * wy)
+            values[n] = (values[n][0] * magnitude, values[n][1] * magnitude)
+        for k, (re, im) in enumerate(slab_dft(values, 1.0)):
+            re, im = rotate(re, im, turn_ref[0, k, rows, :], turn_ref[1, k, rows, :])
+            work_ref[k, rows, :] = re
+            work_ref[k, below, :] = im
+        return carry
+
+    lax.fori_loop(0, long // 8, two, 0)
+
+    def three(k, carry):
+        done = multiply((back_ref[0], back_ref[1]), split(work_ref[k]), PLAIN)
+        out_ref[:, 0, k] = done[:long].reshape(parts, 8, LANES)
+        out_ref[:, 1, k] = done[long:].reshape(parts, 8, LANES)
+        return carry
+
+    lax.fori_loop(0, YS, three, 0)
+
+
+def filter_lines(got, wx_row):
+    parts, _, _, _, rows_x = got.shape
+    long = parts * 8
+    span_y = long * YS
+    cos, sin = phases(YS, long, span_y, 1.0)
+    turn = jnp.broadcast_to(
+        jnp.asarray(np.stack([cos, sin]), jnp.float32)[..., None], (2, YS, long, LANES)
+    )
+    forward = left_table(long, -1.0, 1.0 / math.sqrt(span_y))
+    back = left_table(long, 1.0, 1.0 / math.sqrt(span_y))
+    block = pl.BlockSpec((parts, 2, YS, 8, LANES), lambda i: (0, 0, 0, 0, i))
+    return pl.pallas_call(
+        filter_kernel,
+        grid=(rows_x // LANES,),
+        in_specs=[
+            block,
+            pl.BlockSpec((8, LANES), lambda i: (0, i)),
+            pl.BlockSpec(turn.shape, lambda i: (0, 0, 0, 0)),
+            pl.BlockSpec(forward.shape, lambda i: (0, 0, 0)),
+            pl.BlockSpec(back.shape, lambda i: (0, 0, 0)),
+        ],
+        out_specs=block,
+        out_shape=jax.ShapeDtypeStruct(got.shape, jnp.float32),
+        scratch_shapes=[pltpu.VMEM((YS, 2 * long, LANES), jnp.float32)],
+        compiler_params=pltpu.CompilerParams(vmem_limit_bytes=VMEM_BYTES),
+        name="filter_lines",
+    )(got, wx_row, turn, forward, back)
+
+
+def exchange(values):
+    return lax.all_to_all(values, ("wave", "cfd"), split_axis=0, concat_axis=0, tiled=True)
+
+
+def cut_tiles(grid_values, places):
+    across = grid_values.shape[1] // TILE
+
+    def kernel(place_ref, in_ref, out_ref):
+        out_ref[0] = in_ref[...]
+
+    return pl.pallas_call(
+        kernel,
+        grid_spec=pltpu.PrefetchScalarGridSpec(
+            num_scalar_prefetch=1,
+            grid=(places.shape[0],),
+            in_specs=[
+                pl.BlockSpec((BY, TILE), lambda i, place: (place[i] // across, place[i] % across))
+            ],
+            out_specs=pl.BlockSpec((1, BY, TILE), lambda i, place: (i, 0, 0)),
+        ),
+        out_shape=jax.ShapeDtypeStruct((places.shape[0], BY, TILE), jnp.float32),
+        name="cut_tiles",
+    )(places, grid_values)
+
+
+def blend_kernel(slot_ref, need_ref, gain_ref, upper_ref, level_ref, cfd_ref, out_ref, press_ref):
+    lane = lax.broadcasted_iota(jnp.int32, (BY, TILE), 1)
+    line = lax.broadcasted_iota(jnp.int32, (BY, TILE), 0)
+    ramp = 1.0 - (lane.astype(jnp.float32) + 0.5) / TILE
+
+    def later(value):
+        return jnp.where(lane == TILE - 1, 0.0, pltpu.roll(value, TILE - 1, 1))
+
+    def before(value):
+        return jnp.where(lane == 0, 0.0, pltpu.roll(value, 1, 1))
+
+    def below(value):
+        return jnp.where(line == BY - 1, 0.0, pltpu.roll(value, BY - 1, 0))
+
+    def above(value):
+        return jnp.where(line == 0, 0.0, pltpu.roll(value, 1, 0))
+
+    def one(b, carry):
+        weight = gain_ref[b] * ramp
+        parts = [level_ref[0, need_ref[b]], level_ref[1, need_ref[b]], upper_ref[slot_ref[b]]]
+        mixed = []
+        for c in range(3):
+            value = weight * parts[c] + (1.0 - weight) * cfd_ref[b, c]
+            out_ref[b, c] = value
+            mixed.append(value)
+        u, v = mixed[0], mixed[1]
+        source = (later(u) - before(u)) * 0.5 + (below(v) - above(v)) * 0.5
+        pressure = jnp.zeros_like(source)
+        for sweep in range(SWEEPS):
+            beside = below(pressure) + above(pressure) + later(pressure) + before(pressure)
+            pressure = (beside - source) / 4.5
+        press_ref[b] = pressure
+        return carry
+
+    lax.fori_loop(0, cfd_ref.shape[0], one, 0)
+
+
+def blend_cells(slot_index, cell_need, relax_gain, upper, level, cfd_velocity):
+    scalar = pl.BlockSpec(memory_space=pltpu.SMEM)
+    vector = pl.BlockSpec(memory_space=pltpu.VMEM)
+    return pl.pallas_call(
+        blend_kernel,
+        in_specs=[scalar] * 3 + [vector] * 3,
+        out_specs=[vector] * 2,
+        out_shape=[
+            jax.ShapeDtypeStruct(cfd_velocity.shape, jnp.float32),
+            jax.ShapeDtypeStruct((cfd_velocity.shape[0], BY, TILE), jnp.float32),
+        ],
+        compiler_params=pltpu.CompilerParams(vmem_limit_bytes=VMEM_BYTES),
+        name="blend_cells",
+    )(slot_index, cell_need, relax_gain, upper, level, cfd_velocity)
+
+
+def hull_velocity(spectra, hull_line, hull_point, kx, wave_x, span_x):
+    count = hull_line.shape[0]
+    rows_x = kx.shape[0]
+    lines = hull_line[:, None] + jnp.arange(BY, dtype=jnp.int32)[None, :]
+    owner, within = lines // (8 * YS), lines % (8 * YS)
+    inner = within % YS * 8 + within // YS
+    re_row = (owner * 2) * (8 * YS) + inner
+    rows = jnp.stack([re_row, re_row + 8 * YS]).reshape(-1)
+
+    def picked(values):
+        taken = jnp.take(values.reshape(-1, rows_x), rows, axis=0)
+        taken = taken.reshape(2, count, BY, rows_x)
+        return taken[0], taken[1]
+
+    potential_re, potential_im = picked(spectra[0])
+    across_re, across_im = picked(spectra[1])
+    along_re, along_im = -wave_x * potential_im, wave_x * potential_re
+    field_re = jnp.stack([along_re, across_re])
+    field_im = jnp.stack([along_im, across_im])
+
+    def angle(point):
+        turns = point[:, None] * kx[None, :] % span_x
+        return turns.astype(jnp.float32) * (2.0 * math.pi / span_x)
+
+    start = angle(hull_point)[:, None, :]
+    field_re, field_im = rotate(field_re, field_im, jnp.cos(start), jnp.sin(start))
+    inside = angle(jnp.arange(TILE, dtype=jnp.int32))
+    scaling = 1.0 / math.sqrt(span_x)
+    table = jnp.concatenate([jnp.cos(inside), -jnp.sin(inside)], axis=1) * scaling
+    both = jnp.concatenate([field_re, field_im], axis=-1)
+    return jnp.einsum("fhjr,tr->fhjt", both, table, precision=HIGHEST)
+
+
+def local_fast(phi_spec, elevation, hull_owner, hull_place, cell_need, cfd_velocity, relax_gain):
+    devices = lax.axis_size(("wave", "cfd"))
+    rank_here = lax.axis_index(("wave", "cfd"))
+    rows_x = phi_spec.shape[1]
+    rows_y, span_x = elevation.shape
+    wave_x = wave_numbers(rank_here * rows_x, rows_x, span_x)
+    wx_wide = jnp.broadcast_to(wave_x[:, None], (rows_x, LANES))
+    wx_row = jnp.broadcast_to(wave_x[None, :], (8, rows_x))
+
+    sent = rows_inverse(phi_spec, wx_wide, "vertical", span_x)
+    sent, wx_after = lax.optimization_barrier((sent, wx_wide))
+    got = exchange(sent)
+
+    potential = rows_inverse(phi_spec, wx_after, "potential", span_x)
+    across = rows_inverse(phi_spec, wx_after, "across", span_x)
+    owners = hull_owner[:, 0]
+    hull_blocks = span_x // TILE
+    hull_line = owners * rows_y + hull_place // hull_blocks * BY
+    hull_point = hull_place % hull_blocks * TILE
+    kx = rank_here * rows_x + jnp.arange(rows_x, dtype=jnp.int32)
+    level = hull_velocity((potential, across), hull_line, hull_point, kx, wave_x, span_x)
+    got, level = lax.optimization_barrier((got, level))
+    level = lax.psum(level, ("wave", "cfd"))
+
+    elev = elevation.reshape(8, YS, rows_x, devices).transpose(3, 1, 0, 2)
+    elev = elev.reshape(devices, rows_y, rows_x)
+
+    cos, sin = phases(devices, rows_x, span_x, 1.0)
+    turn = jnp.asarray(np.stack([cos, sin]), jnp.float32)
+    scaling = 1.0 / math.sqrt(span_x)
+    real_table = right_table(rows_x, 1.0, scaling, True)
+    forward_table = right_table(rows_x, -1.0, scaling, False)
+    back_table = right_table(rows_x, 1.0, scaling, False)
+
+    w_first, paired = points_call(
+        first_order_kernel,
+        got.reshape(devices, 2, rows_y, rows_x),
+        [elev],
+        [turn, real_table, forward_table],
+        ["real", "pair"],
+        "first_order",
+    )
+    returned = exchange(paired).reshape(devices, 2, YS, 8, rows_x)
+    filtered = exchange(filter_lines(returned, wx_row))
+    (surface,) = points_call(
+        second_order_kernel,
+        filtered.reshape(devices, 2, rows_y, rows_x),
+        [elev, w_first],
+        [turn, back_table],
+        ["real"],
+        "second_order",
+    )
+    w_surface = surface.reshape(devices, YS, 8, rows_x).transpose(2, 1, 3, 0)
+    w_surface = w_surface.reshape(rows_y, span_x)
+
+    owner_table = (owners[:, None] == jnp.arange(devices, dtype=jnp.int32)[None, :]).astype(
+        jnp.int32
+    )
+    owner_rank = jnp.sum(jnp.cumsum(owner_table, axis=0) * owner_table, axis=1) - 1
+    mine = owners == rank_here
+    capacity = 4 * HULL_DEV
+    select = (
+        mine[None, :] & (owner_rank[None, :] == jnp.arange(capacity, dtype=jnp.int32)[:, None])
+    ).astype(jnp.int32)
+    slot_place = jnp.sum(select * hull_place[None, :], axis=1)
+    tiles = cut_tiles(w_surface, slot_place)
+    gathered = lax.all_gather(tiles, ("wave", "cfd"), axis=0, tiled=True)
+    slot_index = owners[cell_need] * capacity + owner_rank[cell_need]
+    blended, pressure = blend_cells(
+        slot_index, cell_need, relax_gain, gathered, level, cfd_velocity
+    )
+    return (w_surface, blended, pressure)
+
+
+def local(phi_spec, elevation, *others):
+    devices = lax.axis_size(("wave", "cfd"))
+    rows_x, span_y = phi_spec.shape[1:]
+    fits = (
+        devices <= 32
+        and elevation.shape[0] == 8 * YS
+        and rows_x % LANES == 0
+        and span_y // YS % LANES == 0
+    )
+    return (local_fast if fits else local_general)(phi_spec, elevation, *others)
 
 
 def solution(mesh):

time: 1990 us -> 827 us (0.42)
  matrix products: 608 us -> 3.57 us
  waiting for transfers between devices: 827 us -> 323 us
  local copies, waits for them, and re-layouts: 371 us -> 78.9 us
  Pallas kernels: 0 us -> 195 us
  blocking collectives: 0 us -> 191 us
  other arithmetic: 96.2 us -> 7.43 us
  starting transfers between devices: 56.4 us -> 11.5 us
    dot_general x42 -> x1, matrix products: 608 us -> 3.57 us  [hull_velocity(): return jnp.einsum('fhjr,tr->fhjt', both, table, precision=HIGHEST)]
    all_to_all x6 -> x2, waiting for transfers between devices: 764 us -> 266 us  [exchange(): lax.all_to_all(values, ('wave', 'cfd'), split_axis=0, concat_axis=0, tile...]
    pallas_call x0 -> x8, Pallas kernels: none -> 195 us  [the longest x3 79.5 us: rows_inverse(): pl.pallas_call(kernel, grid=(rows_x // LANES,), in_specs=[pl.BlockSpec((2...]
    all_to_all x0 -> x1, blocking collectives: none -> 191 us  [exchange(): lax.all_to_all(values, ('wave', 'cfd'), split_axis=0, concat_axis=0, tile...]
    reshape x7 -> x4, local copies, waits for them, and re-layouts: 125 us -> 34.4 us  [the longest x1 13 us: local_fast(): w_surface = w_surface.reshape(rows_y, span_x)]
    mul x10 -> x0, local copies, waits for them, and re-layouts: 68.5 us -> none  [the longest x1 19.9 us: lines_inverse(): final_re * scaling]
    unnamed x91 -> x22, local copies, waits for them, and re-layouts: 58.7 us -> 1.66 us
    all_to_all x4 -> x0, other arithmetic: 55.7 us -> none  [the longest x1 14.3 us: local(): lax.all_to_all(sent_re, ('wave', 'cfd'), split_axis=0, concat_axis=0, til...]
  transfers between devices with their start and end apart: 7 -> 4, of which waited for: 7 -> 3; matrix products, arithmetic and copies ran while one was open for 17% -> 10% of each run, Pallas kernels for 0% -> 9%
where the time goes in v1:
time: 827 us; the launch traced here: 825 us
  waiting for transfers between devices  323 us (39%)
  Pallas kernels  195 us (24%)
  blocking collectives  191 us (23%)
  local copies, waits for them, and re-layouts  78.9 us (10%)
  between operations  14.3 us (2%)
  starting transfers between devices  11.5 us (1%)
    all_to_all x2, waiting for transfers between devices, exchange(): lax.all_to_all(values, ('wave', 'cfd'), split_axis=0, concat_axis=0, tile...  266 us
    all_to_all x1, blocking collectives, exchange(): lax.all_to_all(values, ('wave', 'cfd'), split_axis=0, concat_axis=0, tile...  191 us
    pallas_call x3, Pallas kernels, rows_inverse(): pl.pallas_call(kernel, grid=(rows_x // LANES,), in_specs=[pl.BlockSpec((2...  79.5 us
    all_gather x1, waiting for transfers between devices, local_fast(): gathered = lax.all_gather(tiles, ('wave', 'cfd'), axis=0, tiled=True)  56.7 us
    pallas_call x1, Pallas kernels, filter_lines(): pl.pallas_call(filter_kernel, grid=(rows_x // LANES,), in_specs=[block, p...  51.6 us
    pallas_call x2, Pallas kernels, points_call(): pl.pallas_call(kernel, grid=(lines // LINES_STEP,), in_specs=[pair_block]...  45.8 us
    gather x2, local copies, waits for them, and re-layouts, picked(): taken = jnp.take(values.reshape(-1, rows_x), rows, axis=0)  22 us
  transfers between devices with their start and end apart: 4, of which 3 were waited for; matrix products, arithmetic and copies ran while one was open for 10% of the time, Pallas kernels for 9%

profile of v1, /device:TPU:0, one launch (start us, length us, event | category | flops | bytes accessed | tf_op | source)
XLA Modules:
  0.0 825.2 jit_solution(15060814616866575633)
XLA Ops:
  7.2 0.6 fusion.39
  7.7 0.6 copy-done.5
  8.3 0.8 broadcast_in_dim.17.refs_1_
  9.1 27.4 %rows_vertical.1 = f32[32,2,16,8,256]{4,3,2,1,0:T(8,128)} custom-call(f32[2,256,4096]{2,1,0:T(8,128)} %refs_0_.5, f32[256,128]{1,0:T(8,128)} %broadcast_in_dim.17.refs_1_, f32[2,16,256]{2,1,0:T(8,128)} %constant.167.clone.refs_2_, bf16[2,512,512]{2,1,0:T(8,128)(2,1)} %constant.168.clone.refs_3_.back_ref), custom_call_target="tpu_custom_call" | custom-call | flops 40000000000 | bytes 16777216 | tf_op jit(solution)/shard_map/rows_vertical/pallas_call | solution.py:359
  36.5 7.4 all-to-all-start
  44.0 0.1 copy.41
  44.2 0.1 reshape.401
  44.3 26.4 %rows_across.1 = f32[32,2,16,8,256]{4,3,2,1,0:T(8,128)} custom-call(f32[2,256,4096]{2,1,0:T(8,128)} %refs_0_.5, f32[256,128]{1,0:T(8,128)} %broadcast_in_dim.17.refs_1_, f32[2,16,256]{2,1,0:T(8,128)} %constant.167.clone.refs_2_, bf16[2,512,512]{2,1,0:T(8,128)(2,1)} %constant.168.clone.refs_3_.back_ref), custom_call_target="tpu_custom_call" | custom-call | flops 40000000000 | bytes 16777216 | tf_op jit(solution)/shard_map/rows_across/pallas_call | solution.py:359
  70.7 10.0 %gather_fusion.3 = f32[2048,256]{1,0:T(8,128)S(1)} fusion(f32[8192,256]{1,0:T(8,128)} %bitcast.34, s32[2048]{0:T(1024)S(1)} %fusion.23), kind=kCustom, calls=%fused_computation.1.clone | custom fusion | bytes 4202496 | tf_op jit(solution)/shard_map/jit(_take)/gather | solution.py:642
  80.7 25.7 %rows_potential.1 = f32[32,2,16,8,256]{4,3,2,1,0:T(8,128)} custom-call(f32[2,256,4096]{2,1,0:T(8,128)} %refs_0_.5, f32[256,128]{1,0:T(8,128)} %broadcast_in_dim.17.refs_1_, f32[2,16,256]{2,1,0:T(8,128)} %constant.167.clone.refs_2_, bf16[2,512,512]{2,1,0:T(8,128)(2,1)} %constant.168.clone.refs_3_.back_ref), custom_call_target="tpu_custom_call" | custom-call | flops 40000000000 | bytes 16777216 | tf_op jit(solution)/shard_map/rows_potential/pallas_call | solution.py:359
  106.4 12.0 %gather_fusion.2 = f32[2048,256]{1,0:T(8,128)} fusion(f32[8192,256]{1,0:T(8,128)} %bitcast.33, s32[2048]{0:T(1024)S(1)} %fusion.23), kind=kCustom, calls=%fused_computation.clone | custom fusion | bytes 4202496 | tf_op jit(solution)/shard_map/jit(_take)/gather | solution.py:642
  118.3 2.8 broadcast_select_fusion.1
  121.1 0.1 slice_bitcast_fusion.2
  121.2 0.3 copy.43
  121.6 1.3 copy.45
  122.9 10.8 %reshape.404 = f32[8,16,256,32]{3,2,1,0:T(8,128)} reshape(f32[128,8192]{1,0:T(8,128)} %param.23) | data formatting | bytes 8388608 | tf_op jit(solution)/shard_map/reshape | solution.py:689
  133.7 11.9 %copy.46 = f32[32,16,8,256]{3,2,1,0:T(8,128)} copy(f32[32,16,8,256]{0,3,1,2:T(8,128)} %bitcast.31) | data formatting | bytes 8388608 | tf_op jit(solution)/shard_map/transpose | solution.py:689
  145.5 1.1 fusion.19
  146.6 0.1 slice_bitcast_fusion.3
  146.8 0.5 copy-done.6
  147.3 0.3 copy_multiply_fusion
  147.6 0.3 copy_multiply_fusion.1
  148.0 0.5 copy-done.3
  148.5 0.6 multiply_subtract_fusion
  149.1 3.6 fusion
  152.7 76.5 %all-to-all-done = f32[32,2,16,8,256]{4,3,2,1,0:T(8,128)} async-done(((f32[32,2,16,8,256]{4,3,2,1,0:T(8,128)}), f32[32,2,16,8,256]{4,3,2,1,0:T(8,128)}, u32[]{:S(2)}, u32[]{:S(2)}) %all-to-all-start) | async-done | bytes 8388640 | tf_op jit(solution)/shard_map/all_to_all | solution.py:555
  229.2 30.1 %first_order.1 = (f32[32,128,256]{2,1,0:T(8,128)}, f32[32,2,128,256]{3,2,1,0:T(8,128)}) custom-call(f32[32,2,128,256]{3,2,1,0:T(8,128)} %bitcast.9.got_ref, f32[32,128,256]{2,1,0:T(8,128)} %bitcast.35, f32[2,32,256]{2,1,0:T(8,128)} %constant.169.clone.turn_ref, bf16[2,512,256]{2,1,0:T(8,128)(2,1)} %constant.170.clone.real_ref, ...), custom_call_target="tpu_custom_call" | custom-call | flops 20000000000 | bytes 20971520 | tf_op jit(solution)/shard_map/first_order/pallas_call | solution.py:451
  259.4 191.0 %all_to_all.15 = f32[32,2,128,256]{3,2,1,0:T(8,128)} all-to-all(f32[32,2,128,256]{3,2,1,0:T(8,128)} %get-tuple-element.15), channel_id=1, replica_groups=mesh['wave'=8,'cfd'=4] {'wave','cfd'}, dimensions={0} | all-to-all | bytes 16777216 | tf_op jit(solution)/shard_map/all_to_all | solution.py:555
  450.3 0.6 broadcast_in_dim.18.wx_ref
  450.9 2.6 broadcast_in_dim.19.turn_ref
  453.5 51.6 %filter_lines.1 = f32[32,2,16,8,256]{4,3,2,1,0:T(8,128)} custom-call(f32[32,2,16,8,256]{4,3,2,1,0:T(8,128)} %bitcast.32, f32[8,256]{1,0:T(8,128)} %broadcast_in_dim.18.wx_ref, f32[2,16,256,128]{3,2,1,0:T(8,128)} %broadcast_in_dim.19.turn_ref, bf16[2,512,512]{2,1,0:T(8,128)(2,1)} %constant.173.clone.forward_ref, ...), custom_call_target="tpu_custom_call" | custom-call | tf_op jit(solution)/shard_map/filter_lines/pallas_call | solution.py:536
  505.1 4.0 all-to-all-start.2
  509.2 0.1 fusion.18
  509.3 0.2 reduce_window_sum.11
  509.4 0.2 select_reduce_fusion
  509.7 0.6 select_reduce_fusion.1.place_ref
  510.3 1.6 copy.48
  511.9 0.0 all-gather.2.cloned.1.call-start
  512.0 189.9 %all-to-all-done.2 = f32[32,2,16,8,256]{4,3,2,1,0:T(8,128)} async-done(((f32[32,2,16,8,256]{4,3,2,1,0:T(8,128)}), f32[32,2,16,8,256]{4,3,2,1,0:T(8,128)}, u32[]{:S(2)}, u32[]{:S(2)}) %all-to-all-start.2) | async-done | bytes 8388640 | tf_op jit(solution)/shard_map/all_to_all | solution.py:555
  701.9 15.6 %second_order.1 = f32[32,128,256]{2,1,0:T(8,128)} custom-call(f32[32,2,128,256]{3,2,1,0:T(8,128)} %bitcast.13.got_ref, f32[32,128,256]{2,1,0:T(8,128)} %bitcast.36, f32[32,128,256]{2,1,0:T(8,128)} %get-tuple-element.16.first_ref, f32[2,32,256]{2,1,0:T(8,128)} %constant.169.clone.turn_ref, bf16[2,512,512]{2,1,0:T(8,128)(2,1)} %constant.172.clone.table_ref), custom_call_target="tpu_custom_call" | custom-call | flops 20000000000 | bytes 20971520 | tf_op jit(solution)/shard_map/second_order/pallas_call | solution.py:451
  717.5 10.5 %copy.47 = f32[32,16,8,256]{0,3,1,2:T(8,128)} copy(f32[32,16,8,256]{3,2,1,0:T(8,128)} %bitcast.37) | data formatting | bytes 8388608 | tf_op jit(solution)/shard_map/reshape | solution.py:717
  728.0 13.0 %reshape.409.in_ref = f32[128,8192]{1,0:T(8,128)} reshape(f32[8,16,256,32]{3,2,1,0:T(8,128)} %bitcast.30) | data formatting | bytes 8388608 | tf_op jit(solution)/shard_map/reshape | solution.py:718
  741.0 6.4 cut_tiles.1
  747.5 0.7 gather_fusion.1
  748.2 0.7 gather_fusion
  748.9 0.6 multiply_add_fusion.1.slot_ref
  749.5 56.7 %all-gather.2.cloned.1.call-done.upper_ref = f32[512,8,128]{2,1,0:T(8,128)} async-done(((f32[16,8,128]{2,1,0:T(8,128)}), f32[512,8,128]{2,1,0:T(8,128)}) %all-gather.2.cloned.1.call-update) | async-done | bytes 2097168 | tf_op jit(solution)/shard_map/all_gather | solution.py:731
  806.2 12.2 %blend_cells.1 = (f32[32,3,8,128]{3,2,1,0:T(8,128)}, f32[32,8,128]{2,1,0:T(8,128)}) custom-call(s32[32]{0:T(128)} %multiply_add_fusion.1.slot_ref, s32[32]{0:T(128)} %need_ref.1, f32[32]{0:T(128)} %gain_ref.1, f32[512,8,128]{2,1,0:T(8,128)} %all-gather.2.cloned.1.call-done.upper_ref, f32[2,128,8,128]{3,2,1,0:T(8,128)} %all-reduce.2.cloned.1.call-done.level_ref, ...), custom_call_target="tpu_custom_call" | custom-call | tf_op jit(solution)/shard_map/blend_cells/pallas_call | solution.py:619
  (33 shorter events, 0.2 us)
Async XLA Ops:
  7.7 0.6 copy-start.5
  36.5 7.4 copy-start
  36.5 7.4 copy-start.8
  36.5 192.7 %all-to-all-start = ((f32[32,2,16,8,256]{4,3,2,1,0:T(8,128)}), f32[32,2,16,8,256]{4,3,2,1,0:T(8,128)}, u32[]{:S(2)}, u32[]{:S(2)}) async-start(f32[32,2,16,8,256]{4,3,2,1,0:T(8,128)} %rows_vertical.1), calls=%async_computation | async-start | bytes 16777216 | tf_op jit(solution)/shard_map/all_to_all | solution.py:555
  133.7 12.9 %copy-start.2 = (f32[2048,256]{1,0:T(8,128)S(1)}, f32[2048,256]{1,0:T(8,128)}, u32[]{:S(2)}) copy-start(f32[2048,256]{1,0:T(8,128)} %get-tuple-element.26) | copy-start | bytes 6291460
  146.6 0.7 copy-start.6
  146.8 0.9 copy-start.7
  147.3 1.2 copy-start.3
  259.4 191.6 %copy-start.4 = (f32[2,16,256]{2,1,0:T(8,128)S(1)}, f32[2,16,256]{2,1,0:T(8,128)}, u32[]{:S(2)}) copy-start(f32[2,16,256]{2,1,0:T(8,128)} %constant.167.clone.refs_2_) | copy-start | bytes 98308
  505.1 4.0 copy-start.1
  505.1 4.5 copy-start.9
  505.1 196.7 %all-to-all-start.2 = ((f32[32,2,16,8,256]{4,3,2,1,0:T(8,128)}), f32[32,2,16,8,256]{4,3,2,1,0:T(8,128)}, u32[]{:S(2)}, u32[]{:S(2)}) async-start(f32[32,2,16,8,256]{4,3,2,1,0:T(8,128)} %filter_lines.1), calls=%async_computation.2 | async-start | bytes 16777216 | tf_op jit(solution)/shard_map/all_to_all | solution.py:555
  509.1 240.3 %all-reduce.2.cloned.1.call-start = ((), (), s32[]{:S(2)}) async-start(), calls=%async_computation.4 | async-start | bytes 2097152 | tf_op jit(solution)/shard_map/psum | solution.py:687
  511.9 294.2 %all-gather.2.cloned.1.call-start = ((), (), s32[]{:S(2)}) async-start(), calls=%async_computation.3 | async-start | bytes 2162688 | tf_op jit(solution)/shard_map/all_gather | solution.py:731
  741.0 6.4 copy-start.10
Sparse Core Ops, SparseCore 0:
  515.2 216.9 all-reduce.1
  747.5 58.5 all-gather.1
